TPU v7x, 512 devices: a whole 4x8x8 slice. The times are simulated.
512 devices in a mesh: rec: 16 (over z, core), frame: 32 (over x, y).
Axes of the slice: x: 4, y: 8, z: 8, core: 2. Of those that a mesh axis runs over, the one named last changes fastest.
Arguments:
- frames: bfloat16 [16, 49152, 256], P('rec', 'frame'), may hold values from -10 to 10
- texts: bfloat16 [32, 224, 256], P('rec', 'frame'), may hold values from -100 to 100
- pair_rec: int32 [32, 1], replicated, may hold values from 0 to 15, as said below
- pair_text: int32 [32], replicated, may hold values from 0 to 31, as said below
- pair_label: int32 [32], replicated, may hold values 0 or 1
Outputs:
- loss: float32 [], replicated
- grad_frames: bfloat16 [16, 49152, 256], P('rec', 'frame')
- grad_texts: bfloat16 [32, 224, 256], P('rec', 'frame')
Inputs may be any that keep to these rules, and one draw needn't show every extreme that they name: `pair_rec`: no recording is named by more than 6 pairs, some recording by exactly 6, and every recording by at least one. A pair's text is held by the index of rec one after, one before, or 8 after its recording (counted round): pair_text // 2 = (pair_rec + k) mod 16 with k one of 1, 15, 8.
All inputs are finite; a program needn't handle non-finite values.
Results may differ from a plain program's by a relative error of at most 0.0085.
Values may be sent and summed in bfloat16 or wider, within the bound.
A program may use at most 64 MiB of HBM per device.

v0:
```python
import jax
import jax.numpy as jnp
from jax import lax
from jax.sharding import PartitionSpec as P

MOST = 6
EPS = 1e-06
TEMP = 10.0
BIAS = -1.0
LOSS_SCALE = 2048.0


def slot_tables(pair_rec, pair_text, pair_label, here, most):
    record = pair_rec[:, 0]
    count = record.shape[0]
    order = jnp.arange(count, dtype=jnp.int32)
    same = (record[:, None] == record[None, :]).astype(jnp.int32)
    earlier = (order[None, :] < order[:, None]).astype(jnp.int32)
    rank = jnp.sum(same * earlier, axis=1)
    places = jnp.arange(most, dtype=jnp.int32)
    chosen = ((record[None, :] == here) & (rank[None, :] == places[:, None])).astype(jnp.int32)
    valid = jnp.sum(chosen, axis=1)
    slot_text = jnp.sum(chosen * pair_text[None, :], axis=1)
    sign = jnp.sum(chosen * (2 * pair_label[None, :] - 1), axis=1)
    return (valid, slot_text, sign)


def pair_terms(score, valid, sign, tokens):
    margin = -sign * (TEMP * score + BIAS)
    loss_part = valid * jax.nn.softplus(margin)
    grad_cos = -LOSS_SCALE * TEMP * valid * sign * jax.nn.sigmoid(margin) / tokens
    return (loss_part, grad_cos)


def body(frames, texts, pair_rec, pair_text, pair_label):
    here = lax.axis_index("rec")
    part = lax.axis_index("frame")
    owned, width_rows, width = texts.shape
    tokens = width_rows * lax.axis_size("frame")
    n_text = owned * lax.axis_size("rec")
    valid, slot_text, sign = slot_tables(pair_rec, pair_text, pair_label, here, MOST)
    valid_f = valid.astype(jnp.float32)
    sign_f = sign.astype(jnp.float32)
    picks = (
        (slot_text[:, None] == jnp.arange(n_text, dtype=jnp.int32)[None, :]) & (valid[:, None] > 0)
    ).astype(jnp.bfloat16)
    whole = lax.all_gather(texts, "frame", axis=1, tiled=True)
    query_vectors = jnp.einsum(
        "jc,cgx->jgx",
        picks,
        lax.all_gather(whole, "rec", axis=0, tiled=True),
        preferred_element_type=jnp.float32,
    ).astype(jnp.bfloat16)
    upstream_signal = frames[0]
    logit_scale = width ** (-0.5)
    pair_scores = (
        jnp.einsum(
            "ype,je->ypj", query_vectors, upstream_signal, preferred_element_type=jnp.float32
        )
        * logit_scale
    )
    local_max = jnp.max(pair_scores, axis=2)
    row_max = lax.pmax(local_max, "frame")
    expo = jnp.exp(pair_scores - row_max[..., None])
    batch_weights = expo.astype(jnp.bfloat16)
    value_partial = jnp.einsum(
        "pqx,xh->pqh", batch_weights, upstream_signal, preferred_element_type=jnp.float32
    )
    query_f = query_vectors.astype(jnp.float32)
    q_norm = lax.rsqrt(jnp.sum(query_f * query_f, axis=2) + EPS)
    q_unit = query_f * q_norm[..., None]
    context = lax.psum(value_partial, "frame")
    c_norm = lax.rsqrt(jnp.sum(context * context, axis=2) + EPS)
    c_unit = context * c_norm[..., None]
    cos = jnp.sum(q_unit * c_unit, axis=2)
    score = jnp.mean(cos, axis=1)
    loss_part, grad_cos = pair_terms(score, valid_f, sign_f, tokens)
    weight = grad_cos[:, None, None]
    d_context = weight * (q_unit - cos[..., None] * c_unit) * c_norm[..., None]
    direct = weight * (c_unit - cos[..., None] * q_unit) * q_norm[..., None]
    direct_own = lax.dynamic_slice_in_dim(direct, part * width_rows, width_rows, 1)
    context_batch_gradient = d_context.astype(jnp.bfloat16)
    weight_gradient = jnp.einsum(
        "ype,je->ypj", context_batch_gradient, upstream_signal, preferred_element_type=jnp.float32
    )
    score_gradient = (expo * weight_gradient * logit_scale).astype(jnp.bfloat16)
    d_query = lax.psum_scatter(
        jnp.einsum(
            "slf,fd->lsd", score_gradient, upstream_signal, preferred_element_type=jnp.float32
        ),
        "frame",
        scatter_dimension=0,
        tiled=True,
    )
    d_query = d_query + jnp.transpose(direct_own, (1, 0, 2))
    text_term = jnp.einsum(
        "st,lsd->tld", picks.astype(jnp.float32), d_query, precision=lax.Precision.HIGHEST
    )
    grad_texts = lax.psum_scatter(text_term, "rec", scatter_dimension=0, tiled=True).astype(
        jnp.bfloat16
    )
    frame_loss_piece = jnp.einsum(
        "cvm,cvz->mz", score_gradient, query_vectors, preferred_element_type=jnp.float32
    )
    frame_loss_piece = frame_loss_piece + jnp.einsum(
        "cvm,cvz->mz", batch_weights, context_batch_gradient, preferred_element_type=jnp.float32
    )
    grad_frames = frame_loss_piece.astype(jnp.bfloat16)[None]
    loss = lax.psum(jnp.sum(loss_part), "rec")
    return (loss, grad_frames, grad_texts)


def solution(mesh):
    return jax.shard_map(
        body,
        mesh=mesh,
        in_specs=(P("rec", "frame", None), P("rec", "frame", None), P(), P(), P()),
        out_specs=(P(), P("rec", "frame", None), P("rec", "frame", None)),
        check_vma=False,
    )
```

profile of v0, /device:TPU:16, one launch (start us, length us, event | category | flops | bytes accessed | tf_op | source)
XLA Modules:
  0.0 644.4 jit_solution(15901261809968272552)
XLA Ops:
  7.2 0.0 copy-start
  7.2 0.0 all-gather.2.cloned.1.call-start
  7.2 49.8 %all_gather.6 = bf16[2,224,256]{2,0,1:T(2,128)(2,1)S(1)} all-gather(bf16[2,7,256]{2,0,1:T(2,128)(2,1)} %param.6), channel_id=1, replica_groups=mesh['rec'=16,'frame'=32] {'frame'}, dimensions={1}, use_global_device_ids=true | all-gather | bytes 236544 | tf_op jit(solution)/shard_map/all_gather | solution.py:47
  57.0 0.7 copy.20
  57.7 0.0 all-gather.2.cloned.1.call-update
  57.8 0.0 all-reduce.5.cloned.1.call-start
  57.8 0.9 select_reduce_fusion
  58.7 0.7 broadcast_compare_fusion.1
  59.4 0.7 multiply_add_fusion
  60.1 1.3 select_reduce_fusion.2
  61.3 0.0 copy-start.9
  61.3 0.0 copy-start.4
  61.4 0.0 copy-start.8
  61.4 43.4 %all-gather.2.cloned.1.call-done = bf16[32,224,256]{2,1,0:T(8,128)(2,1)} async-done(((bf16[2,224,256]{2,1,0:T(8,128)(2,1)}), bf16[32,224,256]{2,1,0:T(8,128)(2,1)}) %all-gather.2.cloned.1.call-update) | async-done | bytes 3670032 | tf_op jit(solution)/shard_map/all_gather | solution.py:51
  104.7 0.0 copy-done.9
  104.7 4.3 fusion.6
  109.0 0.0 copy-done.4
  109.0 0.0 copy-done.8
  109.0 0.0 copy-done
  109.0 4.4 multiply_reduce_fusion
  113.4 71.4 %pmax.7 = f32[6,224]{1,0:T(8,128)S(1)} all-reduce(f32[6,224]{1,0:T(8,128)S(1)} %get-tuple-element.17), channel_id=1, replica_groups=mesh['rec'=16,'frame'=32] {'frame'}, use_global_device_ids=true, to_apply=%region_6.0 | all-reduce | flops 1344 | bytes 10752 | tf_op jit(solution)/shard_map/pmax | solution.py:63
  184.8 4.9 fusion.13
  189.7 2.1 copy.23
  191.7 0.0 all-reduce.5.cloned.1.call-update
  191.8 0.2 reduce-scatter.3.cloned.1.call-start
  192.0 0.7 add_rsqrt_fusion.1
  192.6 157.1 %all-reduce.5.cloned.1.call-done = f32[6,224,256]{2,0,1:T(8,128)} async-done(((f32[6,224,256]{2,0,1:T(8,128)}), f32[6,224,256]{2,0,1:T(8,128)}) %all-reduce.5.cloned.1.call-update) | async-done | bytes 1376272 | tf_op jit(solution)/shard_map/psum | solution.py:72
  349.7 0.0 copy-start.1
  349.7 1.9 multiply_reduce_fusion.1
  351.6 2.4 multiply_reduce_fusion.2
  354.0 0.0 copy-start.3
  354.0 1.4 fusion.44
  355.4 0.0 copy-start.6
  355.4 0.0 copy-done.1
  355.4 1.8 convert_multiply_fusion
  357.2 0.0 copy-done.3
  357.2 0.0 copy-start.2
  357.2 4.9 multiply_convert_fusion
  362.2 0.0 copy-done.6
  362.2 0.0 copy-done.2
  362.2 0.0 copy-start.10
  362.2 1.3 fusion.10
  363.5 0.7 copy-done.10
  364.2 2.1 copy.47
  366.2 0.0 reduce-scatter.3.cloned.1.call-update
  366.2 1.3 dynamic-slice
  368.2 0.7 constant_dynamic-slice_fusion
  368.9 0.7 constant_dynamic-slice_fusion.1
  369.6 0.0 copy-start.11
  369.6 5.7 convolution_bitcast_fusion
  375.2 0.0 copy-done.11
  375.3 0.0 copy-start.5
  375.3 0.0 copy-start.7
  375.3 2.3 fusion.5
  377.6 209.2 %reduce-scatter.3.cloned.1.call-done = f32[7,6,256]{2,1,0:T(8,128)} async-done(((f32[224,6,256]{2,1,0:T(8,128)}), f32[7,6,256]{2,1,0:T(8,128)}) %reduce-scatter.3.cloned.1.call-update) | async-done | bytes 43024 | tf_op jit(solution)/shard_map/reduce_scatter | solution.py:87
  586.9 0.0 copy-done.5
  586.9 0.0 copy-done.7
  586.9 1.3 fusion.27
  588.2 49.1 %all-reduce.6 = (f32[]{:T(128)}, bf16[32,7,256]{2,0,1:T(8,128)(2,1)S(1)}) all-reduce(f32[]{:T(128)} %get-tuple-element.14, f32[32,7,256]{2,0,1:T(8,128)S(1)} %fusion.27), channel_id=1, replica_groups=mesh['rec'=16,'frame'=32] {'rec'}, use_global_device_ids=true, to_apply=%region_11.12 | all-reduce | flops 57345 | bytes 344072 | tf_op jit(solution)/shard_map/psum | solution.py:109
  637.3 0.6 dynamic-slice_convert_fusion
  (2 shorter events, 0.0 us)
Async XLA Ops:
  7.2 101.8 %copy-start = (bf16[1,1536,256]{2,1,0:T(8,128)(2,1)S(1)}, bf16[1,1536,256]{2,1,0:T(8,128)(2,1)}, u32[]{:S(2)}) copy-start(bf16[1,1536,256]{2,1,0:T(8,128)(2,1)} %param.5) | copy-start | bytes 2359300
  7.2 97.5 %all-gather.2.cloned.1.call-start = ((), (), s32[]{:S(2)}) async-start(), calls=%async_computation.1 | async-start | bytes 3899392 | tf_op jit(solution)/shard_map/all_gather | solution.py:51
  57.8 291.9 %all-reduce.5.cloned.1.call-start = ((), (), s32[]{:S(2)}) async-start(), calls=%async_computation.2 | async-start | bytes 3670016 | tf_op jit(solution)/shard_map/psum | solution.py:72
  61.3 43.4 %copy-start.9 = (s32[6]{0:T(128)}, s32[6]{0:T(128)S(1)}, u32[]{:S(2)}) copy-start(s32[6]{0:T(128)S(1)} %get-tuple-element.7) | copy-start | bytes 76
  61.3 47.6 %copy-start.4 = (s32[6]{0:T(128)}, s32[6]{0:T(128)S(1)}, u32[]{:S(2)}) copy-start(s32[6]{0:T(128)S(1)} %get-tuple-element.6) | copy-start | bytes 76
  61.4 47.6 %copy-start.8 = (pred[6]{0:T(512)(128)(4,1)}, pred[6]{0:T(512)(128)(4,1)S(1)}, u32[]{:S(2)}) copy-start(pred[6]{0:T(512)(128)(4,1)S(1)} %broadcast_compare_fusion) | copy-start | bytes 22
  191.8 395.1 %reduce-scatter.3.cloned.1.call-start = ((), (), s32[]{:S(2)}) async-start(), calls=%async_computation.3 | async-start | bytes 1892352 | tf_op jit(solution)/shard_map/reduce_scatter | solution.py:87
  349.7 5.7 copy-start.1
  354.0 3.2 copy-start.3
  355.4 6.8 %copy-start.6 = (f32[6]{0:T(128)}, f32[6]{0:T(128)S(1)}, u32[]{:S(2)}) copy-start(f32[6]{0:T(128)S(1)} %get-tuple-element.13) | copy-start | bytes 76
  357.2 5.0 copy-start.2
  362.2 2.0 copy-start.10
  369.6 5.7 copy-start.11
  375.3 211.6 %copy-start.5 = (s32[6]{0:T(128)S(1)}, s32[6]{0:T(128)}, u32[]{:S(2)}) copy-start(s32[6]{0:T(128)} %copy-done.4) | copy-start | bytes 76
  375.3 211.6 %copy-start.7 = (f32[6]{0:T(128)S(1)}, f32[6]{0:T(128)}, u32[]{:S(2)}) copy-start(f32[6]{0:T(128)} %copy-done.6) | copy-start | bytes 76
Sparse Core Ops, SparseCore 0:
  57.9 46.7 all-gather.1
  191.9 157.7 all-reduce.4
  366.4 220.4 reduce-scatter.2
where the time goes:
time: 645 us; the launch traced here: 644 us
  waiting for transfers between devices  410 us (64%)
  blocking collectives  170 us (26%)
  matrix products  29 us (4%)
  between operations  14.6 us (2%)
  other arithmetic  11.7 us (2%)
  local copies, waits for them, and re-layouts  8.88 us (1%)
    reduce_scatter x1, waiting for transfers between devices, body(): lax.psum_scatter(jnp.einsum('slf,fd->lsd', score_gradient, upstream_signa...  209 us
    psum x1, waiting for transfers between devices, body(): context = lax.psum(value_partial, 'frame')  157 us
    pmax x1, blocking collectives, body(): row_max = lax.pmax(local_max, 'frame')  71.4 us
    all_gather x1, blocking collectives, body(): whole = lax.all_gather(texts, 'frame', axis=1, tiled=True)  49.8 us
    psum x1, blocking collectives, body(): loss = lax.psum(jnp.sum(loss_part), 'rec')  49.1 us
    all_gather x1, waiting for transfers between devices, body(): lax.all_gather(whole, 'rec', axis=0, tiled=True)  43.4 us
  transfers between devices with their start and end apart: 3, of which 3 were waited for; matrix products, arithmetic and copies ran while one was open for 2% of the time, Pallas kernels for 0%

commit v1 on v0

--- a/solution.py
+++ b/solution.py
@@ -8,6 +8,22 @@
 TEMP = 10.0
 BIAS = -1.0
 LOSS_SCALE = 2048.0
+
+
+def product_in_turn(x, axis, dim, term):
+    size, index, rows = (lax.axis_size(axis), lax.axis_index(axis), x.shape[dim])
+    upward = [(i, (i + 1) % size) for i in range(size)]
+    behind = [(i, (i - 1) % size) for i in range(size)]
+    half = size // 2
+    from_left = from_right = x
+    running = term(x, index * rows)
+    for lap in range(1, half + 1):
+        from_left = lax.ppermute(from_left, axis, upward)
+        if lap < size - half:
+            from_right = lax.ppermute(from_right, axis, behind)
+            running = running + term(from_right, (index + lap) % size * rows)
+        running = running + term(from_left, (index - lap) % size * rows)
+    return running
 
 
 def slot_tables(pair_rec, pair_text, pair_label, here, most):
@@ -45,11 +61,16 @@
         (slot_text[:, None] == jnp.arange(n_text, dtype=jnp.int32)[None, :]) & (valid[:, None] > 0)
     ).astype(jnp.bfloat16)
     whole = lax.all_gather(texts, "frame", axis=1, tiled=True)
-    query_vectors = jnp.einsum(
-        "jc,cgx->jgx",
-        picks,
-        lax.all_gather(whole, "rec", axis=0, tiled=True),
-        preferred_element_type=jnp.float32,
+    query_vectors = product_in_turn(
+        whole,
+        "rec",
+        0,
+        lambda part_2, start: jnp.einsum(
+            "jc,cgx->jgx",
+            lax.dynamic_slice_in_dim(picks, start, part_2.shape[0], axis=1),
+            part_2,
+            preferred_element_type=jnp.float32,
+        ),
     ).astype(jnp.bfloat16)
     upstream_signal = frames[0]
     logit_scale = width ** (-0.5)

time: 645 us -> 656 us (1.017)
  waiting for transfers between devices: 410 us -> 386 us
  starting transfers between devices: 0.3 us -> 24.2 us
  matrix products: 29 us -> 42.9 us
    all_gather x1 -> x0, waiting for transfers between devices: 43.4 us -> none  [body(): lax.all_gather(whole, 'rec', axis=0, tiled=True)]
    ppermute x0 -> x15, starting transfers between devices: none -> 24.1 us  [the longest x7 24.1 us: product_in_turn(): from_right = lax.ppermute(from_right, axis, behind)]
    ppermute x0 -> x15, waiting for transfers between devices: none -> 16.9 us  [the longest x8 16.8 us: product_in_turn(): from_left = lax.ppermute(from_left, axis, upward)]
    dot_general x1 -> x16, matrix products: 4.25 us -> 18.3 us  [body(): jnp.einsum('jc,cgx->jgx', lax.dynamic_slice_in_dim(picks, start, part_2.s...]
  transfers between devices with their start and end apart: 3 -> 17, of which waited for: 3 -> 9; matrix products, arithmetic and copies ran while one was open for 2% -> 4% of each run, Pallas kernels for 0% -> 0%
where the time goes in v1:
time: 656 us; the launch traced here: 655 us
  waiting for transfers between devices  386 us (59%)
  blocking collectives  168 us (26%)
  matrix products  42.9 us (7%)
  starting transfers between devices  24.2 us (4%)
  between operations  15.1 us (2%)
  other arithmetic  9.81 us (1%)
  local copies, waits for them, and re-layouts  8.82 us (1%)
    reduce_scatter x1, waiting for transfers between devices, body(): lax.psum_scatter(jnp.einsum('slf,fd->lsd', score_gradient, upstream_signa...  209 us
    psum x1, waiting for transfers between devices, body(): context = lax.psum(value_partial, 'frame')  160 us
    pmax x1, blocking collectives, body(): row_max = lax.pmax(local_max, 'frame')  69.5 us
    all_gather x1, blocking collectives, body(): whole = lax.all_gather(texts, 'frame', axis=1, tiled=True)  49.8 us
    psum x1, blocking collectives, body(): loss = lax.psum(jnp.sum(loss_part), 'rec')  49.1 us
    ppermute x7, starting transfers between devices, product_in_turn(): from_right = lax.ppermute(from_right, axis, behind)  24.1 us
    dot_general x16, matrix products, body(): jnp.einsum('jc,cgx->jgx', lax.dynamic_slice_in_dim(picks, start, part_2.s...  18.3 us
    ppermute x8, waiting for transfers between devices, product_in_turn(): from_left = lax.ppermute(from_left, axis, upward)  16.8 us
  transfers between devices with their start and end apart: 17, of which 9 were waited for; matrix products, arithmetic and copies ran while one was open for 4% of the time, Pallas kernels for 0%

profile of v1, /device:TPU:16, one launch (start us, length us, event | category | flops | bytes accessed | tf_op | source)
XLA Modules:
  0.0 655.5 jit_solution(12194371327748313545)
XLA Ops:
  7.2 0.0 all-reduce.5.cloned.1.call-start
  7.2 49.8 %all_gather.3 = bf16[2,224,256]{2,0,1:T(2,128)(2,1)S(1)} all-gather(bf16[2,7,256]{2,0,1:T(2,128)(2,1)} %param.6), channel_id=1, replica_groups=mesh['rec'=16,'frame'=32] {'frame'}, dimensions={1}, use_global_device_ids=true | all-gather | bytes 236544 | tf_op jit(solution)/shard_map/all_gather | solution.py:63
  57.0 2.9 collective-permute-start
  60.0 0.7 multiply_add_fusion
  60.6 0.7 broadcast_compare_fusion.1
  61.3 0.9 select_reduce_fusion
  62.2 1.3 select_reduce_fusion.2
  63.5 0.5 copy-done.12
  64.1 0.5 fusion.32
  64.6 0.0 collective-permute-start.3
  64.7 6.2 collective-permute-start.2
  70.9 0.5 fusion.38
  71.4 0.5 fusion.35
  71.9 2.7 collective-permute-done.3
  74.6 3.0 collective-permute-start.4
  77.6 0.5 fusion.44
  78.0 0.5 fusion.41
  78.5 2.7 collective-permute-done.5
  81.2 3.0 collective-permute-start.6
  84.2 0.5 fusion.50
  84.7 0.5 fusion.47
  85.2 2.7 collective-permute-done.7
  87.9 3.0 collective-permute-start.8
  90.9 0.5 fusion.56
  91.4 0.5 fusion.53
  91.8 2.7 collective-permute-done.9
  94.5 3.0 collective-permute-start.10
  97.5 0.5 fusion.62
  98.0 0.5 fusion.59
  98.5 2.7 collective-permute-done.11
  101.2 3.0 collective-permute-start.12
  104.2 1.7 fusion.68
  105.9 1.7 fusion.65
  107.7 0.2 collective-permute-done.13
  107.9 1.7 fusion.74
  109.6 1.7 fusion.71
  111.3 3.2 collective-permute-done.14
  114.5 6.0 fusion.4
  120.6 4.5 multiply_reduce_fusion
  125.0 69.5 %pmax.7 = f32[6,224]{1,0:T(8,128)S(1)} all-reduce(f32[6,224]{1,0:T(8,128)S(1)} %get-tuple-element.17), channel_id=1, replica_groups=mesh['rec'=16,'frame'=32] {'frame'}, use_global_device_ids=true, to_apply=%region_6.7 | all-reduce | flops 1344 | bytes 10752 | tf_op jit(solution)/shard_map/pmax | solution.py:84
  194.5 4.9 fusion.8
  199.4 2.1 copy.21
  201.5 0.0 reduce-scatter.3.cloned.1.call-start
  201.5 0.7 add_rsqrt_fusion.1
  202.2 160.2 %all-reduce.5.cloned.1.call-done = f32[6,224,256]{2,0,1:T(8,128)} async-done(((f32[6,224,256]{2,0,1:T(8,128)}), f32[6,224,256]{2,0,1:T(8,128)}) %all-reduce.5.cloned.1.call-update) | async-done | bytes 1376272 | tf_op jit(solution)/shard_map/psum | solution.py:93
  362.4 2.0 multiply_reduce_fusion.1
  364.4 0.1 copy-done.1
  364.4 1.2 multiply_reduce_fusion.2
  365.7 0.6 fusion.80
  366.3 1.8 convert_multiply_fusion
  368.1 5.0 multiply_convert_fusion
  373.1 1.3 fusion.5
  374.3 0.7 copy-done.14
  375.0 2.1 copy.42
  377.1 0.0 reduce-scatter.3.cloned.1.call-update
  377.1 1.4 dynamic-slice
  379.2 0.7 constant_dynamic-slice_fusion.1
  379.9 0.7 constant_dynamic-slice_fusion
  380.6 5.7 convolution_bitcast_fusion
  386.3 2.3 fusion.3
  388.6 209.1 %reduce-scatter.3.cloned.1.call-done = f32[7,6,256]{2,1,0:T(8,128)} async-done(((f32[224,6,256]{2,1,0:T(8,128)}), f32[7,6,256]{2,1,0:T(8,128)}) %reduce-scatter.3.cloned.1.call-update) | async-done | bytes 43024 | tf_op jit(solution)/shard_map/reduce_scatter | solution.py:108
  597.7 1.2 fusion.22
  598.9 49.1 %all-reduce.6 = (f32[]{:T(128)}, bf16[32,7,256]{2,0,1:T(8,128)(2,1)S(1)}) all-reduce(f32[]{:T(128)} %get-tuple-element.14, f32[32,7,256]{2,0,1:T(8,128)S(1)} %fusion.22), channel_id=1, replica_groups=mesh['rec'=16,'frame'=32] {'rec'}, use_global_device_ids=true, to_apply=%region_11.12 | all-reduce | flops 57345 | bytes 344072 | tf_op jit(solution)/shard_map/psum | solution.py:130
  648.0 0.6 dynamic-slice_convert_fusion
  (48 shorter events, 0.2 us)
Async XLA Ops:
  7.2 113.4 %copy-start = (bf16[1,1536,256]{2,1,0:T(8,128)(2,1)S(1)}, bf16[1,1536,256]{2,1,0:T(8,128)(2,1)}, u32[]{:S(2)}) copy-start(bf16[1,1536,256]{2,1,0:T(8,128)(2,1)} %param.5) | copy-start | bytes 2359300
  7.2 355.2 %all-reduce.5.cloned.1.call-start = ((), (), s32[]{:S(2)}) async-start(), calls=%async_computation.1 | async-start | bytes 3670016 | tf_op jit(solution)/shard_map/psum | solution.py:93
  57.0 7.6 %collective-permute-start.1 = (bf16[2,224,256]{2,0,1:T(2,128)(2,1)S(1)}, bf16[2,224,256]{2,0,1:T(2,128)(2,1)S(1)}, u32[]{:S(2)}, u32[]{:S(2)}) collective-permute-start(bf16[2,224,256]{2,0,1:T(2,128)(2,1)S(1)} %all_gather.3), channel_id=1, source_target_pairs={{0,32},{32,64},{64,96},{96,128},{128,160},{160,192},{192,224},{224... | collective-permute-start | bytes 688136 | tf_op jit(solution)/shard_map/ppermute | solution.py:21
  57.0 7.6 %collective-permute-start = (bf16[2,224,256]{2,0,1:T(2,128)(2,1)S(1)}, bf16[2,224,256]{2,0,1:T(2,128)(2,1)S(1)}, u32[]{:S(2)}, u32[]{:S(2)}) collective-permute-start(bf16[2,224,256]{2,0,1:T(2,128)(2,1)S(1)} %all_gather.3), channel_id=1, source_target_pairs={{0,480},{32,0},{64,32},{96,64},{128,96},{160,128},{192,160},{224,1... | collective-permute-start | bytes 688136 | tf_op jit(solution)/shard_map/ppermute | solution.py:23
  63.5 0.5 copy-start.12
  63.5 7.9 %copy-start.8 = (s32[6]{0:T(128)}, s32[6]{0:T(128)S(1)}, u32[]{:S(2)}) copy-start(s32[6]{0:T(128)S(1)} %get-tuple-element.6) | copy-start | bytes 76
  64.0 7.4 %copy-start.10 = (pred[6]{0:T(512)(128)(4,1)}, pred[6]{0:T(512)(128)(4,1)S(1)}, u32[]{:S(2)}) copy-start(pred[6]{0:T(512)(128)(4,1)S(1)} %broadcast_compare_fusion) | copy-start | bytes 22
  64.6 9.9 %collective-permute-start.3 = (bf16[2,224,256]{2,0,1:T(2,128)(2,1)S(1)}, bf16[2,224,256]{2,0,1:T(2,128)(2,1)S(1)}, u32[]{:S(2)}, u32[]{:S(2)}) collective-permute-start(bf16[2,224,256]{2,0,1:T(2,128)(2,1)S(1)} %collective-permute-done.1), channel_id=1, source_target_pairs={{0,32},{32,64},{64,96},{96,128},{128,160},{160,192},{192,224},{224... | collective-permute-start | bytes 688136 | tf_op jit(solution)/shard_map/ppermute | solution.py:21
  64.7 9.9 %collective-permute-start.2 = (bf16[2,224,256]{2,0,1:T(2,128)(2,1)S(1)}, bf16[2,224,256]{2,0,1:T(2,128)(2,1)S(1)}, u32[]{:S(2)}, u32[]{:S(2)}) collective-permute-start(bf16[2,224,256]{2,0,1:T(2,128)(2,1)S(1)} %collective-permute-done), channel_id=1, source_target_pairs={{0,480},{32,0},{64,32},{96,64},{128,96},{160,128},{192,160},{224,1... | collective-permute-start | bytes 688136 | tf_op jit(solution)/shard_map/ppermute | solution.py:23
  74.6 6.7 %collective-permute-start.5 = (bf16[2,224,256]{2,0,1:T(2,128)(2,1)S(1)}, bf16[2,224,256]{2,0,1:T(2,128)(2,1)S(1)}, u32[]{:S(2)}, u32[]{:S(2)}) collective-permute-start(bf16[2,224,256]{2,0,1:T(2,128)(2,1)S(1)} %collective-permute-done.3), channel_id=1, source_target_pairs={{0,32},{32,64},{64,96},{96,128},{128,160},{160,192},{192,224},{224... | collective-permute-start | bytes 688136 | tf_op jit(solution)/shard_map/ppermute | solution.py:21
  74.6 6.7 %collective-permute-start.4 = (bf16[2,224,256]{2,0,1:T(2,128)(2,1)S(1)}, bf16[2,224,256]{2,0,1:T(2,128)(2,1)S(1)}, u32[]{:S(2)}, u32[]{:S(2)}) collective-permute-start(bf16[2,224,256]{2,0,1:T(2,128)(2,1)S(1)} %collective-permute-done.2), channel_id=1, source_target_pairs={{0,480},{32,0},{64,32},{96,64},{128,96},{160,128},{192,160},{224,1... | collective-permute-start | bytes 688136 | tf_op jit(solution)/shard_map/ppermute | solution.py:23
  81.2 6.7 %collective-permute-start.7 = (bf16[2,224,256]{2,0,1:T(2,128)(2,1)S(1)}, bf16[2,224,256]{2,0,1:T(2,128)(2,1)S(1)}, u32[]{:S(2)}, u32[]{:S(2)}) collective-permute-start(bf16[2,224,256]{2,0,1:T(2,128)(2,1)S(1)} %collective-permute-done.5), channel_id=1, source_target_pairs={{0,32},{32,64},{64,96},{96,128},{128,160},{160,192},{192,224},{224... | collective-permute-start | bytes 688136 | tf_op jit(solution)/shard_map/ppermute | solution.py:21
  81.2 6.7 %collective-permute-start.6 = (bf16[2,224,256]{2,0,1:T(2,128)(2,1)S(1)}, bf16[2,224,256]{2,0,1:T(2,128)(2,1)S(1)}, u32[]{:S(2)}, u32[]{:S(2)}) collective-permute-start(bf16[2,224,256]{2,0,1:T(2,128)(2,1)S(1)} %collective-permute-done.4), channel_id=1, source_target_pairs={{0,480},{32,0},{64,32},{96,64},{128,96},{160,128},{192,160},{224,1... | collective-permute-start | bytes 688136 | tf_op jit(solution)/shard_map/ppermute | solution.py:23
  87.9 6.7 %collective-permute-start.9 = (bf16[2,224,256]{2,0,1:T(2,128)(2,1)S(1)}, bf16[2,224,256]{2,0,1:T(2,128)(2,1)S(1)}, u32[]{:S(2)}, u32[]{:S(2)}) collective-permute-start(bf16[2,224,256]{2,0,1:T(2,128)(2,1)S(1)} %collective-permute-done.7), channel_id=1, source_target_pairs={{0,32},{32,64},{64,96},{96,128},{128,160},{160,192},{192,224},{224... | collective-permute-start | bytes 688136 | tf_op jit(solution)/shard_map/ppermute | solution.py:21
  87.9 6.7 %collective-permute-start.8 = (bf16[2,224,256]{2,0,1:T(2,128)(2,1)S(1)}, bf16[2,224,256]{2,0,1:T(2,128)(2,1)S(1)}, u32[]{:S(2)}, u32[]{:S(2)}) collective-permute-start(bf16[2,224,256]{2,0,1:T(2,128)(2,1)S(1)} %collective-permute-done.6), channel_id=1, source_target_pairs={{0,480},{32,0},{64,32},{96,64},{128,96},{160,128},{192,160},{224,1... | collective-permute-start | bytes 688136 | tf_op jit(solution)/shard_map/ppermute | solution.py:23
  94.5 6.7 %collective-permute-start.11 = (bf16[2,224,256]{2,0,1:T(2,128)(2,1)S(1)}, bf16[2,224,256]{2,0,1:T(2,128)(2,1)S(1)}, u32[]{:S(2)}, u32[]{:S(2)}) collective-permute-start(bf16[2,224,256]{2,0,1:T(2,128)(2,1)S(1)} %collective-permute-done.9), channel_id=1, source_target_pairs={{0,32},{32,64},{64,96},{96,128},{128,160},{160,192},{192,224},{224... | collective-permute-start | bytes 688136 | tf_op jit(solution)/shard_map/ppermute | solution.py:21
  94.5 6.7 %collective-permute-start.10 = (bf16[2,224,256]{2,0,1:T(2,128)(2,1)S(1)}, bf16[2,224,256]{2,0,1:T(2,128)(2,1)S(1)}, u32[]{:S(2)}, u32[]{:S(2)}) collective-permute-start(bf16[2,224,256]{2,0,1:T(2,128)(2,1)S(1)} %collective-permute-done.8), channel_id=1, source_target_pairs={{0,480},{32,0},{64,32},{96,64},{128,96},{160,128},{192,160},{224,1... | collective-permute-start | bytes 688136 | tf_op jit(solution)/shard_map/ppermute | solution.py:23
  101.2 6.7 %collective-permute-start.13 = (bf16[2,224,256]{2,0,1:T(2,128)(2,1)S(1)}, bf16[2,224,256]{2,0,1:T(2,128)(2,1)S(1)}, u32[]{:S(2)}, u32[]{:S(2)}) collective-permute-start(bf16[2,224,256]{2,0,1:T(2,128)(2,1)S(1)} %collective-permute-done.11), channel_id=1, source_target_pairs={{0,32},{32,64},{64,96},{96,128},{128,160},{160,192},{192,224},{224... | collective-permute-start | bytes 688136 | tf_op jit(solution)/shard_map/ppermute | solution.py:21
  101.2 8.4 %collective-permute-start.12 = (bf16[2,224,256]{2,0,1:T(2,128)(2,1)S(1)}, bf16[2,224,256]{2,0,1:T(2,128)(2,1)S(1)}, u32[]{:S(2)}, u32[]{:S(2)}) collective-permute-start(bf16[2,224,256]{2,0,1:T(2,128)(2,1)S(1)} %collective-permute-done.10), channel_id=1, source_target_pairs={{0,480},{32,0},{64,32},{96,64},{128,96},{160,128},{192,160},{224,1... | collective-permute-start | bytes 688136 | tf_op jit(solution)/shard_map/ppermute | solution.py:23
  107.9 6.7 %collective-permute-start.14 = (bf16[2,224,256]{2,0,1:T(2,128)(2,1)S(1)}, bf16[2,224,256]{2,0,1:T(2,128)(2,1)S(1)}, u32[]{:S(2)}, u32[]{:S(2)}) collective-permute-start(bf16[2,224,256]{2,0,1:T(2,128)(2,1)S(1)} %collective-permute-done.13), channel_id=1, source_target_pairs={{0,32},{32,64},{64,96},{96,128},{128,160},{160,192},{192,224},{224... | collective-permute-start | bytes 688136 | tf_op jit(solution)/shard_map/ppermute | solution.py:21
  199.4 2.2 copy-start.5
  201.5 396.2 %reduce-scatter.3.cloned.1.call-start = ((), (), s32[]{:S(2)}) async-start(), calls=%async_computation.2 | async-start | bytes 1892352 | tf_op jit(solution)/shard_map/reduce_scatter | solution.py:108
  362.4 2.1 copy-start.1
  362.4 2.1 copy-start.2
  364.4 1.2 copy-start.11
  364.4 1.2 copy-start.13
  365.6 2.4 copy-start.4
  366.3 1.8 copy-start.6
  368.1 5.0 copy-start.3
  373.1 2.0 copy-start.14
  380.6 5.7 copy-start.15
  386.3 211.5 %copy-start.7 = (f32[6]{0:T(128)S(1)}, f32[6]{0:T(128)}, u32[]{:S(2)}) copy-start(f32[6]{0:T(128)} %copy-done.6) | copy-start | bytes 76
  386.3 211.5 %copy-start.9 = (s32[6]{0:T(128)S(1)}, s32[6]{0:T(128)}, u32[]{:S(2)}) copy-start(s32[6]{0:T(128)} %copy-done.8) | copy-start | bytes 76
Sparse Core Ops, SparseCore 0:
  201.6 160.7 all-reduce.4
  377.2 220.4 reduce-scatter.2
